TPU v7x, 32 devices: a whole 2x2x4 slice. The times are simulated.
32 devices in a mesh: win: 2 (over y), blk: 4 (over z), smp: 4 (over x, core).
Axes of the slice: x: 2, y: 2, z: 4, core: 2. Of those that a mesh axis runs over, the one named last changes fastest.
Arguments:
- dosage: bfloat16 [65536, 1024], P(('win', 'smp'), 'blk'), parts along dimension 0, may hold values from 0 to 2
- allele_counts: int32 [2048], P(('win', 'blk')), parts along dimension 0, may hold values from 19660 to 45875
- keep: float32 [2048], P(('win', 'blk')), parts along dimension 0, may hold values from 0.5 to 1
- reach: int32 [8], P(('win', 'blk')), parts along dimension 0, may hold values from 0 to 2, as said below
Outputs:
- ld_band: float32 [8, 5, 256, 256], P(('win', 'blk'), None, 'smp'), parts along dimension 0
There are 2 independent parts, one for each index of `win`. A program takes and returns all parts, laid end to end along the dimension named above; each array names one. Nothing has to cross between parts.
Inputs may be any that keep to these rules, and one draw needn't show every extreme that they name: Some block has reach 2 and some block has reach 0.
All inputs are finite; a program needn't handle non-finite values.
Results may differ from a plain program's by a relative error of at most 0.00055.
Values may be sent and summed in bfloat16 or wider, within the bound.
A program may use at most 64 MiB of HBM per device.

v0:
```python
import jax
import jax.numpy as jnp
from jax import lax
from jax.sharding import PartitionSpec as P

H = 2


def shifted(block, axis, distance):
    devices = range(lax.axis_size(axis))
    route = [(i - distance, i) for i in devices if i - distance in devices]
    return lax.ppermute(block, axis, route)


def standardize(dosage, allele_counts, keep, total):
    freq = (allele_counts.astype(jnp.float32) + 1.0) / (2.0 * total + 2.0)
    factor = keep * lax.rsqrt(2.0 * freq * (1.0 - freq))
    return ((dosage.astype(jnp.float32) - 2.0 * freq) * factor).astype(jnp.bfloat16)


def gram_of(left_cols, right_cols):
    return lax.dot_general(
        left_cols, right_cols, (((0,), (0,)), ((), ())), preferred_element_type=jnp.float32
    )


def on_device(dosage, allele_counts, keep, reach):
    samples_local, block_width = dosage.shape
    n_smp = lax.axis_size("smp")
    n_blk = lax.axis_size("blk")
    sample_total = samples_local * n_smp
    scaled = standardize(dosage, allele_counts, keep, sample_total)
    row_count = block_width // n_smp
    row_start = lax.axis_index("smp") * row_count
    block_index = lax.axis_index("blk")
    own_reach = reach[0]
    keep_rows = lax.dynamic_slice_in_dim(keep, row_start, row_count, 0)
    row_ids = lax.broadcasted_iota(jnp.int32, (row_count, block_width), 0) + row_start
    col_ids = lax.broadcasted_iota(jnp.int32, (row_count, block_width), 1)
    diag_term = jnp.where(
        row_ids == col_ids, (1.0 - keep_rows * keep_rows)[:, None], jnp.float32(0.0)
    )
    ahead = [shifted(scaled, "blk", -distance) for distance in range(1, H + 1)]
    partners = jnp.concatenate([scaled] + ahead, axis=1)
    validity = [
        (distance <= own_reach) & (block_index + distance < n_blk) for distance in range(H + 1)
    ]
    band_slots = [None] * (2 * H + 1)
    transposes = []
    summed = lax.psum(gram_of(scaled, partners), "smp") / sample_total
    for distance in range(H + 1):
        segment = summed[:, distance * block_width : (distance + 1) * block_width]
        owned_rows = lax.dynamic_slice_in_dim(segment, row_start, row_count, 0)
        band_slots[H + distance] = jnp.where(validity[distance], owned_rows, jnp.float32(0.0))
        if distance > 0:
            transposes.append(lax.dynamic_slice_in_dim(segment, row_start, row_count, 1).T)
    for distance in range(1, H + 1):
        returned_part = jnp.where(validity[distance], transposes[distance - 1], jnp.float32(0.0))
        band_slots[H - distance] = shifted(
            returned_part.astype(jnp.bfloat16), "blk", distance
        ).astype(returned_part.dtype)
    band_slots[H] = band_slots[H] + diag_term
    return jnp.stack(band_slots, axis=0)[None]


def solution(mesh):
    in_specs = (P(("win", "smp"), "blk"), P(("win", "blk")), P(("win", "blk")), P(("win", "blk")))
    out_specs = P(("win", "blk"), None, "smp", None)
    return jax.shard_map(
        on_device, mesh=mesh, in_specs=in_specs, out_specs=out_specs, check_vma=False
    )
```

profile of v0, /device:TPU:0, one launch (start us, length us, event | category | flops | bytes accessed | tf_op | source)
XLA Modules:
  0.0 343.2 jit_solution(2893275606810973559)
XLA Ops:
  6.5 0.7 fusion.8
  7.2 3.3 multiply_convert_fusion
  10.5 0.0 copy-start.1
  10.5 1.3 collective-permute-start.1
  11.8 1.3 collective-permute-start
  13.1 184.0 %collective-permute-done.1 = bf16[8192,256]{1,0:T(8,128)(2,1)S(1)} collective-permute-done((bf16[8192,256]{1,0:T(8,128)(2,1)S(1)}, bf16[8192,256]{1,0:T(8,128)(2,1)S(1)}, u32[]{:S(2)}, u32[]{:S(2)}) %collective-permute-start.1) | collective-permute-done | bytes 4194336 | tf_op jit(solution)/shard_map/ppermute | solution.py:12
  197.1 0.0 collective-permute-done
  197.1 4.4 %fusion = f32[256,768]{1,0:T(8,128)} fusion(bf16[8192,256]{1,0:T(8,128)(2,1)S(1)} %multiply_convert_fusion, bf16[8192,256]{1,0:T(8,128)(2,1)S(1)} %collective-permute-done.1, bf16[8192,256]{1,0:T(8,128)(2,1)S(1)} %collective-permute-done), kind=kOutput, calls=%fused_computation | convolution fusion | flops 3258974208 | bytes 13369344 | tf_op jit(solution)/shard_map/dot_general | solution.py:22
  201.5 0.0 all-reduce.2.cloned.1.call-update
  202.3 0.1 multiply_subtract_fusion
  202.3 122.0 %all-reduce.2.cloned.1.call-done = f32[256,768]{1,0:T(8,128)} async-done(((f32[256,768]{1,0:T(8,128)}), f32[256,768]{1,0:T(8,128)}) %all-reduce.2.cloned.1.call-update) | async-done | bytes 786448 | tf_op jit(solution)/shard_map/psum | solution.py:50
  324.3 1.2 broadcast_multiply_fusion
  325.5 0.1 fusion.10
  325.5 0.1 fusion.6
  325.7 4.3 %collective-permute-start.2 = (bf16[64,256]{0,1:T(8,128)(2,1)S(1)}, bf16[64,256]{0,1:T(8,128)(2,1)S(1)}, u32[]{:S(2)}, u32[]{:S(2)}) collective-permute-start(bf16[64,256]{0,1:T(8,128)(2,1)S(1)} %fusion.6), channel_id=1, source_target_pairs={{0,8},{4,12},{1,9},{5,13},{2,10},{6,14},{3,11},{7,15},{16,24},{20,... | collective-permute-start | bytes 98312 | tf_op jit(solution)/shard_map/ppermute | solution.py:12
  330.0 0.1 fusion.7
  330.1 3.4 collective-permute-start.3
  333.5 0.0 collective-permute-done.2
  333.5 0.1 copy.5
  333.6 1.8 collective-permute-done.3
  335.4 0.1 copy.6
  335.5 0.1 bitcast_dynamic-update-slice_fusion.2
  335.6 0.0 copy-start
  335.6 0.7 copy-done
  (9 shorter events, 0.1 us)
Async XLA Ops:
  6.5 317.8 %all-reduce.2.cloned.1.call-start = ((), (), s32[]{:S(2)}) async-start(), calls=%async_computation | async-start | bytes 1572864 | tf_op jit(solution)/shard_map/psum | solution.py:50
  10.5 191.7 %copy-start.1 = (f32[256]{0:T(256)S(1)}, f32[256]{0:T(256)}, u32[]{:S(2)}) copy-start(f32[256]{0:T(256)} %param.6) | copy-start | bytes 3076
  10.5 186.6 %collective-permute-start.1 = (bf16[8192,256]{1,0:T(8,128)(2,1)S(1)}, bf16[8192,256]{1,0:T(8,128)(2,1)S(1)}, u32[]{:S(2)}, u32[]{:S(2)}) collective-permute-start(bf16[8192,256]{1,0:T(8,128)(2,1)S(1)} %multiply_convert_fusion), channel_id=1, source_target_pairs={{8,0},{12,4},{9,1},{13,5},{10,2},{14,6},{11,3},{15,7},{24,16},{28,... | collective-permute-start | bytes 12582920 | tf_op jit(solution)/shard_map/ppermute | solution.py:12
  11.8 185.3 %collective-permute-start = (bf16[8192,256]{1,0:T(8,128)(2,1)S(1)}, bf16[8192,256]{1,0:T(8,128)(2,1)S(1)}, u32[]{:S(2)}, u32[]{:S(2)}) collective-permute-start(bf16[8192,256]{1,0:T(8,128)(2,1)S(1)} %multiply_convert_fusion), channel_id=1, source_target_pairs={{4,0},{8,4},{12,8},{5,1},{9,5},{13,9},{6,2},{10,6},{14,10},{7,3},{... | collective-permute-start | bytes 12582920 | tf_op jit(solution)/shard_map/ppermute | solution.py:12
  325.7 7.8 %collective-permute-start.2 = (bf16[64,256]{0,1:T(8,128)(2,1)S(1)}, bf16[64,256]{0,1:T(8,128)(2,1)S(1)}, u32[]{:S(2)}, u32[]{:S(2)}) collective-permute-start(bf16[64,256]{0,1:T(8,128)(2,1)S(1)} %fusion.6), channel_id=1, source_target_pairs={{0,8},{4,12},{1,9},{5,13},{2,10},{6,14},{3,11},{7,15},{16,24},{20,... | collective-permute-start | bytes 98312 | tf_op jit(solution)/shard_map/ppermute | solution.py:12
  330.1 5.3 %collective-permute-start.3 = (bf16[64,256]{0,1:T(8,128)(2,1)S(1)}, bf16[64,256]{0,1:T(8,128)(2,1)S(1)}, u32[]{:S(2)}, u32[]{:S(2)}) collective-permute-start(bf16[64,256]{0,1:T(8,128)(2,1)S(1)} %fusion.7), channel_id=1, source_target_pairs={{0,4},{4,8},{8,12},{1,5},{5,9},{9,13},{2,6},{6,10},{10,14},{3,7},{... | collective-permute-start | bytes 98312 | tf_op jit(solution)/shard_map/ppermute | solution.py:12
  335.6 0.7 copy-start
Sparse Core Ops, SparseCore 0:
  201.7 122.5 all-reduce.1
where the time goes:
time: 343 us
  waiting for transfers between devices  308 us (90%)
  between operations  14.2 us (4%)
  starting transfers between devices  10.3 us (3%)
  other arithmetic  5.57 us (2%)
  matrix products  4.42 us (1%)
    ppermute x4, waiting for transfers between devices, shifted(): return lax.ppermute(block, axis, route)  186 us
    psum x1, waiting for transfers between devices, on_device(): summed = lax.psum(gram_of(scaled, partners), 'smp') / sample_total  122 us
    ppermute x4, starting transfers between devices, shifted(): return lax.ppermute(block, axis, route)  10.3 us
  transfers between devices with their start and end apart: 5, of which 3 were waited for; matrix products, arithmetic and copies ran while one was open for 0% of the time, Pallas kernels for 0%

commit v1 on v0

v1 whole, which is shorter than its diff:
```python
import functools

import jax
import jax.numpy as jnp
from jax import lax
from jax.experimental import pallas as pl
from jax.experimental.pallas import tpu as pltpu
from jax.sharding import PartitionSpec as P

H = 2
CHUNKS = 8
MESH = pl.DeviceIdType.MESH


def gram_of(left_cols, right_cols):
    return lax.dot_general(
        left_cols, right_cols, (((0,), (0,)), ((), ())), preferred_element_type=jnp.float32
    )


def kernel(
    n_blk, n_smp, total,
    counts_ref, keep_ref, reach_ref, dosage_ref, out_ref,
    raw, own, left, right, reach_out, reach_in,
    diag, diag_in, acc, acc_in, rows_out, rows_in, tiles_out, tiles_in, back_out, back_in,
    load_sem, data_send, data_recv, reach_sem, diag_sem, acc_sem, last_sem, rows_sem,
    tiles_sem, back_sem,
):
    z = lax.axis_index("blk")
    s = lax.axis_index("smp")
    rows, width = out_ref.shape[2], out_ref.shape[3]
    chunk = raw.shape[1]
    peers = range(1, n_smp)
    hub = (z >= 1) & (z <= n_blk - 2)
    last_hub = z == n_blk - 2
    hub_above = z <= n_blk - 3
    hub_below = z >= 2

    def remote(src, dst, send_sem, recv_sem, **where):
        return pltpu.make_async_remote_copy(
            src_ref=src, dst_ref=dst, send_sem=send_sem, recv_sem=recv_sem,
            device_id=where, device_id_type=MESH,
        )

    def load(k):
        return pltpu.make_async_copy(
            dosage_ref.at[pl.ds(k * chunk, chunk)], raw.at[k], load_sem.at[k]
        )

    def data_up(k):
        return remote(own.at[k], left.at[k], data_send.at[0, k], data_recv.at[0, k], blk=z + 1)

    def data_down(k):
        return remote(own.at[k], right.at[k], data_send.at[1, k], data_recv.at[1, k], blk=z - 1)

    def reach_up():
        return remote(reach_out, reach_in, reach_sem.at[0], reach_sem.at[1], blk=z + 1)

    def peer_of(d):
        return lax.rem(s + d, n_smp)

    def diag_to(d):
        p = peer_of(d)
        return remote(
            diag.at[pl.ds(p * rows, rows)], diag_in.at[d - 1],
            diag_sem.at[0, d - 1], diag_sem.at[1, d - 1], smp=p,
        )

    def acc_to(d):
        p = peer_of(d)
        return remote(
            acc.at[pl.ds(0, 2), pl.ds(p * rows, rows)], acc_in.at[d - 1, pl.ds(0, 2)],
            acc_sem.at[0, d - 1], acc_sem.at[1, d - 1], smp=p,
        )

    def last_to(d):
        p = peer_of(d)
        return remote(
            acc.at[2, pl.ds(p * rows, rows)], acc_in.at[d - 1, 2],
            last_sem.at[0, d - 1], last_sem.at[1, d - 1], smp=p,
        )

    def tiles_to(d):
        p = peer_of(d)
        return remote(
            tiles_out.at[p], tiles_in.at[s],
            tiles_sem.at[0, d - 1], tiles_sem.at[1, d - 1], smp=p,
        )

    def rows_down():
        return remote(rows_out.at[pl.ds(0, 2)], rows_in, rows_sem.at[0], rows_sem.at[1], blk=z - 1)

    def back_up(j):
        return remote(
            back_out.at[j], back_in.at[j], back_sem.at[0, j], back_sem.at[1, j], blk=z + 1
        )

    for k in range(CHUNKS):
        load(k).start()

    barrier = pltpu.get_barrier_semaphore()
    for d in peers:
        pl.semaphore_signal(barrier, inc=1, device_id={"smp": peer_of(d)}, device_id_type=MESH)

    @pl.when(z > 0)
    def _():
        pl.semaphore_signal(barrier, inc=1, device_id={"blk": z - 1}, device_id_type=MESH)

    @pl.when(z < n_blk - 1)
    def _():
        pl.semaphore_signal(barrier, inc=1, device_id={"blk": z + 1}, device_id_type=MESH)

    keep = keep_ref[...]
    freq = (counts_ref[...].astype(jnp.float32) + 1.0) / (2.0 * total + 2.0)
    factor = keep * lax.rsqrt(2.0 * freq * (1.0 - freq))
    centre = 2.0 * freq
    reach_out[...] = jnp.full(reach_out.shape, reach_ref[0], jnp.int32).astype(jnp.float32)

    def standardize(k):
        load(k).wait()
        own[k] = ((raw[k].astype(jnp.float32) - centre) * factor).astype(jnp.bfloat16)

    def send(k):
        @pl.when(hub_above)
        def _():
            data_up(k).start()

        @pl.when(hub_below)
        def _():
            data_down(k).start()

    standardize(0)
    neighbours = (z > 0).astype(jnp.int32) + (z < n_blk - 1).astype(jnp.int32)
    pl.semaphore_wait(barrier, n_smp - 1 + neighbours)
    send(0)

    @pl.when(hub_above)
    def _():
        reach_up().start()

    @pl.loop(1, CHUNKS)
    def _(k):
        standardize(k)
        send(k)

    diag[...] = jnp.zeros_like(diag)

    @pl.loop(0, CHUNKS)
    def _(k):
        diag[...] += gram_of(own[k], own[k])

    for d in peers:
        diag_to(d).start()

    zero = jnp.zeros((rows, width), jnp.float32)

    @pl.when(hub)
    def _():
        acc[...] = jnp.zeros_like(acc)

        @pl.loop(0, CHUNKS)
        def _(k):
            data_up(k).wait_recv()
            acc[0] += gram_of(left[k], own[k])
            data_down(k).wait_recv()
            acc[1] += gram_of(left[k], right[k])

            @pl.when(last_hub)
            def _():
                acc[2] += gram_of(own[k], right[k])

        for d in peers:
            acc_to(d).start()

        @pl.when(last_hub)
        def _():
            for d in peers:
                last_to(d).start()

        reach_up().wait_recv()

    mine = pl.ds(s * rows, rows)
    for d in peers:
        diag_to(d).wait()
    diag_sum = diag[mine]
    for d in peers:
        diag_sum += diag_in[d - 1]
    row_ids = lax.broadcasted_iota(jnp.int32, (rows, width), 0) + s * rows
    col_ids = lax.broadcasted_iota(jnp.int32, (rows, width), 1)
    out_ref[0, H] = diag_sum / total + jnp.where(row_ids == col_ids, 1.0 - keep * keep, 0.0)

    @pl.when(hub)
    def _():
        def finish(j, limit):
            summed = acc[j, mine]
            for d in peers:
                summed += acc_in[d - 1, j]
            listed = limit[0:1, 0:1]
            summed = jnp.where(listed, summed / total, 0.0)
            rows_out[j] = summed
            turned = summed.T
            for p in range(n_smp):
                tiles_out[p, j] = turned[p * rows : (p + 1) * rows]

        for d in peers:
            acc_to(d).wait()
        finish(0, reach_in[...] >= 1.0)
        finish(1, reach_in[...] >= 2.0)
        rows_down().start()

        @pl.when(last_hub)
        def _():
            for d in peers:
                last_to(d).wait()
            finish(2, reach_out[...] >= 1.0)

        @pl.when(jnp.logical_not(last_hub))
        def _():
            tiles_out[:, 2] = jnp.zeros((n_smp, rows, rows), jnp.float32)

        for d in peers:
            tiles_to(d).start()
        tiles_in[s] = tiles_out[s]
        for d in peers:
            tiles_to(d).wait()

        def gathered(j):
            return jnp.concatenate([tiles_in[q, j] for q in range(n_smp)], axis=1)

        back_out[0] = gathered(1)
        back_up(0).start()

        @pl.when(last_hub)
        def _():
            back_out[1] = gathered(2)
            back_up(1).start()

        out_ref[0, H - 1] = gathered(0)

    @pl.when(hub_above)
    def _():
        rows_down().wait_recv()
        out_ref[0, H + 1] = rows_in[0]
        out_ref[0, H + 2] = rows_in[1]

    @pl.when(last_hub)
    def _():
        out_ref[0, H + 1] = rows_out[2]
        out_ref[0, H + 2] = zero

    @pl.when(z == n_blk - 1)
    def _():
        out_ref[0, H + 1] = zero
        out_ref[0, H + 2] = zero
        back_up(1).wait_recv()
        out_ref[0, H - 1] = back_in[1]

    @pl.when(z == 0)
    def _():
        out_ref[0, H - 1] = zero

    @pl.when(hub_below)
    def _():
        back_up(0).wait_recv()
        out_ref[0, H - 2] = back_in[0]

    @pl.when(jnp.logical_not(hub_below))
    def _():
        out_ref[0, H - 2] = zero

    @pl.when(hub_above)
    def _():
        reach_up().wait_send()

        @pl.loop(0, CHUNKS)
        def _(k):
            data_up(k).wait_send()

    @pl.when(hub_below)
    def _():
        @pl.loop(0, CHUNKS)
        def _(k):
            data_down(k).wait_send()

    @pl.when(hub)
    def _():
        rows_down().wait_send()
        back_up(0).wait_send()

        @pl.when(last_hub)
        def _():
            back_up(1).wait_send()


def solution(mesh):
    n_blk, n_smp = mesh.shape["blk"], mesh.shape["smp"]

    def on_device(dosage, allele_counts, keep, reach):
        samples, width = dosage.shape
        rows = width // n_smp
        chunk = samples // CHUNKS
        block = (CHUNKS, chunk, width)
        f32, bf16 = jnp.float32, jnp.bfloat16
        dma = pltpu.SemaphoreType.DMA
        vmem = pl.BlockSpec(memory_space=pltpu.VMEM)
        return pl.pallas_call(
            functools.partial(kernel, n_blk, n_smp, samples * n_smp),
            out_shape=jax.ShapeDtypeStruct((1, 2 * H + 1, rows, width), f32),
            in_specs=[vmem, vmem, pl.BlockSpec(memory_space=pltpu.SMEM),
                      pl.BlockSpec(memory_space=pl.ANY)],
            out_specs=vmem,
            scratch_shapes=[
                pltpu.VMEM(block, bf16),
                pltpu.VMEM(block, bf16),
                pltpu.VMEM(block, bf16),
                pltpu.VMEM(block, bf16),
                pltpu.VMEM((8, 128), f32),
                pltpu.VMEM((8, 128), f32),
                pltpu.VMEM((width, width), f32),
                pltpu.VMEM((n_smp - 1, rows, width), f32),
                pltpu.VMEM((3, width, width), f32),
                pltpu.VMEM((n_smp - 1, 3, rows, width), f32),
                pltpu.VMEM((3, rows, width), f32),
                pltpu.VMEM((2, rows, width), f32),
                pltpu.VMEM((n_smp, 3, rows, rows), f32),
                pltpu.VMEM((n_smp, 3, rows, rows), f32),
                pltpu.VMEM((2, rows, width), f32),
                pltpu.VMEM((2, rows, width), f32),
                dma((CHUNKS,)),
                dma((2, CHUNKS)),
                dma((2, CHUNKS)),
                dma((2,)),
                dma((2, n_smp - 1)),
                dma((2, n_smp - 1)),
                dma((2, n_smp - 1)),
                dma((2,)),
                dma((2, n_smp - 1)),
                dma((2, 2)),
            ],
            compiler_params=pltpu.CompilerParams(
                collective_id=0, has_side_effects=True, vmem_limit_bytes=40 << 20
            ),
        )(allele_counts[None], keep[None], reach, dosage)

    in_specs = (P(("win", "smp"), "blk"), P(("win", "blk")), P(("win", "blk")), P(("win", "blk")))
    out_specs = P(("win", "blk"), None, "smp", None)
    return jax.shard_map(
        on_device, mesh=mesh, in_specs=in_specs, out_specs=out_specs, check_vma=False
    )
```

time: 343 us -> 120 us (0.35)
  the two profiles are of different devices: /device:TPU:0 before, /device:TPU:27 now
where the time goes in v1:
time: 120 us
  Pallas kernels  115 us (96%)
  local copies, waits for them, and re-layouts  4.26 us (4%)
    pallas_call x1, Pallas kernels, on_device(): pl.pallas_call(functools.partial(kernel, n_blk, n_smp, samples * n_smp),...  115 us
    unnamed x7, local copies, waits for them, and re-layouts  4.26 us

profile of v1, /device:TPU:27, one launch (start us, length us, event | category | flops | bytes accessed | tf_op | source)
XLA Modules:
  0.0 119.7 jit_solution(411943259176972714)
XLA Ops:
  0.7 0.0 copy-start
  0.7 2.2 %copy-done = bf16[8192,256]{1,0:T(8,128)(2,1)S(1)} copy-done((bf16[8192,256]{1,0:T(8,128)(2,1)S(1)}, bf16[8192,256]{1,0:T(8,128)(2,1)}, u32[]{:S(2)}) %copy-start) | copy-done | bytes 4194328
  2.8 0.0 copy-start.1
  2.8 0.7 copy-done.1
  3.5 0.0 copy-start.2
  3.5 0.7 copy-done.2
  4.2 114.8 %shard_map.46 = f32[1,5,64,256]{3,2,1,0:T(8,128)S(1)} custom-call(s32[1,256]{1,0:T(1,128)S(1)} %bitcast.2, f32[1,256]{1,0:T(1,128)S(1)} %bitcast.3, s32[1]{0:T(128)S(6)} %copy.6.reach_ref, bf16[8192,256]{1,0:T(8,128)(2,1)S(1)} %copy-done), custom_call_target="tpu_custom_call" | custom-call | tf_op jit(solution)/shard_map/pallas_call | solution.py:306
  119.0 0.7 copy.7
Async XLA Ops:
  0.7 2.2 %copy-start = (bf16[8192,256]{1,0:T(8,128)(2,1)S(1)}, bf16[8192,256]{1,0:T(8,128)(2,1)}, u32[]{:S(2)}) copy-start(bf16[8192,256]{1,0:T(8,128)(2,1)} %dosage_ref.1) | copy-start | bytes 12582916
  2.8 0.7 copy-start.1
  3.5 0.7 copy-start.2

commit v2 on v1

v2 whole, which is shorter than its diff:
```python
import functools

import jax
import jax.numpy as jnp
from jax import lax
from jax.experimental import pallas as pl
from jax.experimental.pallas import tpu as pltpu
from jax.sharding import PartitionSpec as P

H = 2
CHUNKS = 16
LATE = 3
MESH = pl.DeviceIdType.MESH


def gram_of(left_cols, right_cols):
    return lax.dot_general(
        left_cols, right_cols, (((0,), (0,)), ((), ())), preferred_element_type=jnp.float32
    )


def kernel(
    n_blk, n_smp, total,
    counts_hbm, keep_hbm, reach_hbm, dosage_ref, out_ref,
    counts_ref, keep_ref, reach_ref, raw, own, left, right, reach_out, reach_in,
    diag, diag_in, acc, acc_in, late, late_out, late_in, rows_out, rows_in,
    tiles_out, tiles_in, back_out, back_in,
    meta_sem, load_sem, data_send, data_recv, reach_sem, diag_sem, acc_sem, late_sem, rows_sem,
    tiles_sem, back_sem,
):
    z = lax.axis_index("blk")
    s = lax.axis_index("smp")
    rows, width = out_ref.shape[2], out_ref.shape[3]
    chunk = raw.shape[1]
    early = CHUNKS - LATE
    peers = range(1, n_smp)
    above = z <= n_blk - 2
    below = z >= 1
    inner = above & below
    inner_above = z <= n_blk - 3
    inner_below = z >= 2

    def remote(src, dst, send_sem, recv_sem, **where):
        return pltpu.make_async_remote_copy(
            src_ref=src, dst_ref=dst, send_sem=send_sem, recv_sem=recv_sem,
            device_id=where, device_id_type=MESH,
        )

    def load(k):
        return pltpu.make_async_copy(
            dosage_ref.at[pl.ds(k * chunk, chunk)], raw.at[k], load_sem.at[k]
        )

    def data_up(k):
        return remote(own.at[k], left.at[k], data_send.at[0, k], data_recv.at[0, k], blk=z + 1)

    def data_down(k):
        return remote(own.at[k], right.at[k], data_send.at[1, k], data_recv.at[1, k], blk=z - 1)

    def reach_up():
        return remote(reach_out, reach_in, reach_sem.at[0], reach_sem.at[1], blk=z + 1)

    def peer_of(d):
        return lax.rem(s + d, n_smp)

    def diag_to(d):
        p = peer_of(d)
        return remote(
            diag.at[pl.ds(p * rows, rows)], diag_in.at[d - 1],
            diag_sem.at[0, d - 1], diag_sem.at[1, d - 1], smp=p,
        )

    def acc_to(j, d):
        p = peer_of(d)
        return remote(
            acc.at[j, pl.ds(p * rows, rows)], acc_in.at[j, d - 1],
            acc_sem.at[0, j, d - 1], acc_sem.at[1, j, d - 1], smp=p,
        )

    def late_to(j, d):
        p = peer_of(d)
        return remote(
            late_out.at[j, pl.ds(p * rows, rows)], late_in.at[j, d - 1],
            late_sem.at[0, j, d - 1], late_sem.at[1, j, d - 1], smp=p,
        )

    def rows_down(j):
        return remote(
            rows_out.at[j], rows_in.at[j], rows_sem.at[0, j], rows_sem.at[1, j], blk=z - 1
        )

    def tiles_to(d):
        p = peer_of(d)
        return remote(
            tiles_out.at[p], tiles_in.at[s],
            tiles_sem.at[0, d - 1], tiles_sem.at[1, d - 1], smp=p,
        )

    def back_to(d):
        p = peer_of(d)
        return remote(
            back_out.at[p], back_in.at[s],
            back_sem.at[0, d], back_sem.at[1, d], blk=z + 1, smp=p,
        )

    metas = [
        pltpu.make_async_copy(src, dst, meta_sem.at[i])
        for i, (src, dst) in enumerate(
            [(counts_hbm, counts_ref), (keep_hbm, keep_ref), (reach_hbm, reach_ref)]
        )
    ]
    for copy in metas:
        copy.start()

    @pl.loop(0, CHUNKS)
    def _(k):
        load(k).start()

    barrier = pltpu.get_barrier_semaphore()

    def greet(**where):
        pl.semaphore_signal(barrier, inc=1, device_id=where, device_id_type=MESH)

    for d in peers:
        greet(smp=peer_of(d))

    @pl.when(above)
    def _():
        for d in range(n_smp):
            greet(blk=z + 1, smp=peer_of(d))

    @pl.when(below)
    def _():
        for d in range(n_smp):
            greet(blk=z - 1, smp=peer_of(d))

    for copy in metas:
        copy.wait()
    keep = keep_ref[...]
    freq = (counts_ref[...].astype(jnp.float32) + 1.0) / (2.0 * total + 2.0)
    factor = keep * lax.rsqrt(2.0 * freq * (1.0 - freq))
    centre = 2.0 * freq
    reach_out[...] = jnp.full(reach_out.shape, reach_ref[0], jnp.int32).astype(jnp.float32)

    def standardize(k):
        load(k).wait()
        own[k] = ((raw[k].astype(jnp.float32) - centre) * factor).astype(jnp.bfloat16)

    def send(k):
        @pl.when(above)
        def _():
            data_up(k).start()

        @pl.when(inner_below)
        def _():
            data_down(k).start()

    standardize(0)
    neighbours = above.astype(jnp.int32) + below.astype(jnp.int32)
    pl.semaphore_wait(barrier, n_smp - 1 + n_smp * neighbours)
    send(0)

    @pl.loop(1, CHUNKS)
    def _(k):
        standardize(k)
        send(k)

    @pl.when(above)
    def _():
        reach_up().start()

    diag[...] = jnp.zeros_like(diag)

    @pl.loop(0, CHUNKS)
    def _(k):
        diag[...] += gram_of(own[k], own[k])

    for d in peers:
        diag_to(d).start()

    zero = jnp.zeros((rows, width), jnp.float32)
    acc[...] = jnp.zeros_like(acc)
    late[...] = jnp.zeros_like(late)

    def pairs(k, sums):
        data_up(k).wait_recv()
        sums[0] += gram_of(left[k], own[k])

        @pl.when(inner)
        def _():
            data_down(k).wait_recv()
            sums[1] += gram_of(left[k], right[k])

    @pl.when(below)
    def _():
        @pl.loop(0, early)
        def _(k):
            pairs(k, acc)

        for d in peers:
            acc_to(0, d).start()

        @pl.when(inner)
        def _():
            for d in peers:
                acc_to(1, d).start()

        reach_up().wait_recv()

    mine = pl.ds(s * rows, rows)
    for d in peers:
        diag_to(d).wait()
    diag_sum = diag[mine]
    for d in peers:
        diag_sum += diag_in[d - 1]
    row_ids = lax.broadcasted_iota(jnp.int32, (rows, width), 0) + s * rows
    col_ids = lax.broadcasted_iota(jnp.int32, (rows, width), 1)
    out_ref[0, H] = diag_sum / total + jnp.where(row_ids == col_ids, 1.0 - keep * keep, 0.0)

    def early_sum(j):
        for d in peers:
            acc_to(j, d).wait()
        summed = acc[j, mine]
        for d in peers:
            summed += acc_in[j, d - 1]
        acc[j, mine] = summed

    def late_sum(j):
        summed = acc[j, mine] + late[j, mine]
        for d in peers:
            late_to(j, d).wait()
            summed += late_in[j, d - 1].astype(jnp.float32)
        listed = reach_in[0:1, 0:1] >= j + 1.0
        summed = jnp.where(listed, summed / total, 0.0)
        rows_out[j] = summed
        rows_down(j).start()
        return summed.T.astype(jnp.bfloat16)

    def gathered(tiles):
        return jnp.concatenate(
            [tiles[q].astype(jnp.float32) for q in range(n_smp)], axis=1
        )

    @pl.when(below)
    def _():
        @pl.loop(early, CHUNKS)
        def _(k):
            pairs(k, late)

        late_out[0] = late[0].astype(jnp.bfloat16)
        for d in peers:
            late_to(0, d).start()

        @pl.when(inner)
        def _():
            late_out[1] = late[1].astype(jnp.bfloat16)
            for d in peers:
                late_to(1, d).start()
            early_sum(1)

        early_sum(0)
        turned = late_sum(0)
        for p in range(n_smp):
            tiles_out[p] = turned[p * rows : (p + 1) * rows]
        for d in peers:
            tiles_to(d).start()
        tiles_in[s] = tiles_out[s]

        @pl.when(inner)
        def _():
            turned = late_sum(1)
            for p in range(n_smp):
                back_out[p] = turned[p * rows : (p + 1) * rows]
            for d in range(n_smp):
                back_to(d).start()

        for d in peers:
            tiles_to(d).wait()
        out_ref[0, H - 1] = gathered(tiles_in)

    @pl.when(jnp.logical_not(below))
    def _():
        out_ref[0, H - 1] = zero

    @pl.when(above)
    def _():
        rows_down(0).wait_recv()
        out_ref[0, H + 1] = rows_in[0]

    @pl.when(jnp.logical_not(above))
    def _():
        out_ref[0, H + 1] = zero

    @pl.when(inner_above)
    def _():
        rows_down(1).wait_recv()
        out_ref[0, H + 2] = rows_in[1]

    @pl.when(jnp.logical_not(inner_above))
    def _():
        out_ref[0, H + 2] = zero

    @pl.when(inner_below)
    def _():
        for d in range(n_smp):
            back_to(d).wait_recv()
        out_ref[0, H - 2] = gathered(back_in)

    @pl.when(jnp.logical_not(inner_below))
    def _():
        out_ref[0, H - 2] = zero

    @pl.when(above)
    def _():
        reach_up().wait_send()

        @pl.loop(0, CHUNKS)
        def _(k):
            data_up(k).wait_send()

    @pl.when(inner_below)
    def _():
        @pl.loop(0, CHUNKS)
        def _(k):
            data_down(k).wait_send()

    @pl.when(below)
    def _():
        rows_down(0).wait_send()

    @pl.when(inner)
    def _():
        rows_down(1).wait_send()
        for d in range(n_smp):
            back_to(d).wait_send()


def solution(mesh):
    n_blk, n_smp = mesh.shape["blk"], mesh.shape["smp"]

    def on_device(dosage, allele_counts, keep, reach):
        samples, width = dosage.shape
        rows = width // n_smp
        chunk = samples // CHUNKS
        block = (CHUNKS, chunk, width)
        f32, bf16 = jnp.float32, jnp.bfloat16
        dma = pltpu.SemaphoreType.DMA
        hbm = pl.BlockSpec(memory_space=pl.ANY)
        return pl.pallas_call(
            functools.partial(kernel, n_blk, n_smp, samples * n_smp),
            out_shape=jax.ShapeDtypeStruct((1, 2 * H + 1, rows, width), f32),
            in_specs=[hbm] * 4,
            out_specs=pl.BlockSpec(memory_space=pltpu.VMEM),
            scratch_shapes=[
                pltpu.VMEM((1, width), jnp.int32),
                pltpu.VMEM((1, width), f32),
                pltpu.SMEM((1,), jnp.int32),
                pltpu.VMEM(block, bf16),
                pltpu.VMEM(block, bf16),
                pltpu.VMEM(block, bf16),
                pltpu.VMEM(block, bf16),
                pltpu.VMEM((8, 128), f32),
                pltpu.VMEM((8, 128), f32),
                pltpu.VMEM((width, width), f32),
                pltpu.VMEM((n_smp - 1, rows, width), f32),
                pltpu.VMEM((2, width, width), f32),
                pltpu.VMEM((2, n_smp - 1, rows, width), f32),
                pltpu.VMEM((2, width, width), f32),
                pltpu.VMEM((2, width, width), bf16),
                pltpu.VMEM((2, n_smp - 1, rows, width), bf16),
                pltpu.VMEM((2, rows, width), f32),
                pltpu.VMEM((2, rows, width), f32),
                pltpu.VMEM((n_smp, rows, rows), bf16),
                pltpu.VMEM((n_smp, rows, rows), bf16),
                pltpu.VMEM((n_smp, rows, rows), bf16),
                pltpu.VMEM((n_smp, rows, rows), bf16),
                dma((3,)),
                dma((CHUNKS,)),
                dma((2, CHUNKS)),
                dma((2, CHUNKS)),
                dma((2,)),
                dma((2, n_smp - 1)),
                dma((2, 2, n_smp - 1)),
                dma((2, 2, n_smp - 1)),
                dma((2, 2)),
                dma((2, n_smp - 1)),
                dma((2, n_smp)),
            ],
            compiler_params=pltpu.CompilerParams(
                collective_id=0, has_side_effects=True, vmem_limit_bytes=40 << 20
            ),
        )(allele_counts[None], keep[None], reach, dosage)

    in_specs = (P(("win", "smp"), "blk"), P(("win", "blk")), P(("win", "blk")), P(("win", "blk")))
    out_specs = P(("win", "blk"), None, "smp", None)
    return jax.shard_map(
        on_device, mesh=mesh, in_specs=in_specs, out_specs=out_specs, check_vma=False
    )
```

time: 120 us -> 112 us (0.933)
  the two profiles are of different devices: /device:TPU:27 before, /device:TPU:0 now
where the time goes in v2:
time: 112 us
  Pallas kernels  107 us (96%)
  local copies, waits for them, and re-layouts  4.26 us (4%)
    pallas_call x1, Pallas kernels, on_device(): pl.pallas_call(functools.partial(kernel, n_blk, n_smp, samples * n_smp),...  107 us
    unnamed x7, local copies, waits for them, and re-layouts  4.26 us

profile of v2, /device:TPU:0, one launch (start us, length us, event | category | flops | bytes accessed | tf_op | source)
XLA Modules:
  0.0 112.0 jit_solution(16359890100210373423)
XLA Ops:
  0.7 0.0 copy-start
  0.7 2.2 %copy-done = bf16[8192,256]{1,0:T(8,128)(2,1)S(1)} copy-done((bf16[8192,256]{1,0:T(8,128)(2,1)S(1)}, bf16[8192,256]{1,0:T(8,128)(2,1)}, u32[]{:S(2)}) %copy-start) | copy-done | bytes 4194328
  2.8 0.0 copy-start.1
  2.8 0.7 copy-done.1
  3.5 0.0 copy-start.2
  3.5 0.7 copy-done.2
  4.2 107.1 %shard_map.46 = f32[1,5,64,256]{3,2,1,0:T(8,128)S(1)} custom-call(s32[1,256]{1,0:T(1,128)S(1)} %bitcast.2, f32[1,256]{1,0:T(1,128)S(1)} %bitcast.3, s32[1]{0:T(128)S(6)} %copy.6.reach_hbm, bf16[8192,256]{1,0:T(8,128)(2,1)S(1)} %copy-done), custom_call_target="tpu_custom_call" | custom-call | tf_op jit(solution)/shard_map/pallas_call | solution.py:349
  111.3 0.7 copy.7
Async XLA Ops:
  0.7 2.2 %copy-start = (bf16[8192,256]{1,0:T(8,128)(2,1)S(1)}, bf16[8192,256]{1,0:T(8,128)(2,1)}, u32[]{:S(2)}) copy-start(bf16[8192,256]{1,0:T(8,128)(2,1)} %dosage_ref.1) | copy-start | bytes 12582916
  2.8 0.7 copy-start.1
  3.5 0.7 copy-start.2

commit v3 on v2

--- a/solution.py
+++ b/solution.py
@@ -23,10 +23,9 @@
     n_blk, n_smp, total,
     counts_hbm, keep_hbm, reach_hbm, dosage_ref, out_ref,
     counts_ref, keep_ref, reach_ref, raw, own, left, right, reach_out, reach_in,
-    diag, diag_in, acc, acc_in, late, late_out, late_in, rows_out, rows_in,
-    tiles_out, tiles_in, back_out, back_in,
+    diag, diag_in, acc, acc_in, late, late_out, late_in, rows_out, rows_in, tiles_out, tiles_in,
     meta_sem, load_sem, data_send, data_recv, reach_sem, diag_sem, acc_sem, late_sem, rows_sem,
-    tiles_sem, back_sem,
+    tiles_sem,
 ):
     z = lax.axis_index("blk")
     s = lax.axis_index("smp")
@@ -84,23 +83,14 @@
             late_sem.at[0, j, d - 1], late_sem.at[1, j, d - 1], smp=p,
         )
 
-    def rows_down(j):
-        return remote(
-            rows_out.at[j], rows_in.at[j], rows_sem.at[0, j], rows_sem.at[1, j], blk=z - 1
-        )
-
-    def tiles_to(d):
+    def rows_down():
+        return remote(rows_out, rows_in, rows_sem.at[0], rows_sem.at[1], blk=z - 1)
+
+    def tiles_up(j, d):
         p = peer_of(d)
         return remote(
-            tiles_out.at[p], tiles_in.at[s],
-            tiles_sem.at[0, d - 1], tiles_sem.at[1, d - 1], smp=p,
-        )
-
-    def back_to(d):
-        p = peer_of(d)
-        return remote(
-            back_out.at[p], back_in.at[s],
-            back_sem.at[0, d], back_sem.at[1, d], blk=z + 1, smp=p,
+            tiles_out.at[j, p], tiles_in.at[j, s],
+            tiles_sem.at[0, j, d], tiles_sem.at[1, j, d], blk=z + 1, smp=p,
         )
 
     metas = [
@@ -147,11 +137,11 @@
         own[k] = ((raw[k].astype(jnp.float32) - centre) * factor).astype(jnp.bfloat16)
 
     def send(k):
-        @pl.when(above)
+        @pl.when(inner_above)
         def _():
             data_up(k).start()
 
-        @pl.when(inner_below)
+        @pl.when(below)
         def _():
             data_down(k).start()
 
@@ -165,7 +155,7 @@
         standardize(k)
         send(k)
 
-    @pl.when(above)
+    @pl.when(inner_above)
     def _():
         reach_up().start()
 
@@ -183,15 +173,15 @@
     late[...] = jnp.zeros_like(late)
 
     def pairs(k, sums):
-        data_up(k).wait_recv()
-        sums[0] += gram_of(left[k], own[k])
-
-        @pl.when(inner)
-        def _():
-            data_down(k).wait_recv()
+        data_down(k).wait_recv()
+        sums[0] += gram_of(own[k], right[k])
+
+        @pl.when(inner)
+        def _():
+            data_up(k).wait_recv()
             sums[1] += gram_of(left[k], right[k])
 
-    @pl.when(below)
+    @pl.when(above)
     def _():
         @pl.loop(0, early)
         def _(k):
@@ -204,8 +194,7 @@
         def _():
             for d in peers:
                 acc_to(1, d).start()
-
-        reach_up().wait_recv()
+            reach_up().wait_recv()
 
     mine = pl.ds(s * rows, rows)
     for d in peers:
@@ -225,92 +214,91 @@
             summed += acc_in[j, d - 1]
         acc[j, mine] = summed
 
-    def late_sum(j):
+    def late_sum(j, limit):
         summed = acc[j, mine] + late[j, mine]
         for d in peers:
             late_to(j, d).wait()
             summed += late_in[j, d - 1].astype(jnp.float32)
-        listed = reach_in[0:1, 0:1] >= j + 1.0
-        summed = jnp.where(listed, summed / total, 0.0)
-        rows_out[j] = summed
-        rows_down(j).start()
-        return summed.T.astype(jnp.bfloat16)
-
-    def gathered(tiles):
+        summed = jnp.where(limit[0:1, 0:1] >= j + 1.0, summed / total, 0.0)
+        return summed
+
+    def return_tiles(j, summed):
+        turned = summed.T.astype(jnp.bfloat16)
+        for p in range(n_smp):
+            tiles_out[j, p] = turned[p * rows : (p + 1) * rows]
+        for d in range(n_smp):
+            tiles_up(j, d).start()
+
+    def gathered(j):
+        for d in range(n_smp):
+            tiles_up(j, d).wait_recv()
         return jnp.concatenate(
-            [tiles[q].astype(jnp.float32) for q in range(n_smp)], axis=1
-        )
-
-    @pl.when(below)
+            [tiles_in[j, q].astype(jnp.float32) for q in range(n_smp)], axis=1
+        )
+
+    @pl.when(jnp.logical_not(above))
+    def _():
+        out_ref[0, H + 1] = zero
+
+    @pl.when(jnp.logical_not(inner_above))
+    def _():
+        out_ref[0, H + 2] = zero
+
+    @pl.when(jnp.logical_not(below))
+    def _():
+        out_ref[0, H - 1] = zero
+
+    @pl.when(jnp.logical_not(inner_below))
+    def _():
+        out_ref[0, H - 2] = zero
+
+    @pl.when(above)
     def _():
         @pl.loop(early, CHUNKS)
         def _(k):
             pairs(k, late)
 
-        late_out[0] = late[0].astype(jnp.bfloat16)
-        for d in peers:
-            late_to(0, d).start()
-
         @pl.when(inner)
         def _():
             late_out[1] = late[1].astype(jnp.bfloat16)
             for d in peers:
                 late_to(1, d).start()
+
+        late_out[0] = late[0].astype(jnp.bfloat16)
+        for d in peers:
+            late_to(0, d).start()
+
+        @pl.when(inner)
+        def _():
             early_sum(1)
 
         early_sum(0)
-        turned = late_sum(0)
-        for p in range(n_smp):
-            tiles_out[p] = turned[p * rows : (p + 1) * rows]
-        for d in peers:
-            tiles_to(d).start()
-        tiles_in[s] = tiles_out[s]
-
-        @pl.when(inner)
-        def _():
-            turned = late_sum(1)
-            for p in range(n_smp):
-                back_out[p] = turned[p * rows : (p + 1) * rows]
-            for d in range(n_smp):
-                back_to(d).start()
-
-        for d in peers:
-            tiles_to(d).wait()
-        out_ref[0, H - 1] = gathered(tiles_in)
-
-    @pl.when(jnp.logical_not(below))
-    def _():
-        out_ref[0, H - 1] = zero
-
-    @pl.when(above)
-    def _():
-        rows_down(0).wait_recv()
-        out_ref[0, H + 1] = rows_in[0]
-
-    @pl.when(jnp.logical_not(above))
-    def _():
-        out_ref[0, H + 1] = zero
+
+        @pl.when(inner)
+        def _():
+            summed = late_sum(1, reach_in)
+            rows_out[...] = summed
+            rows_down().start()
+            return_tiles(1, summed)
+
+        summed = late_sum(0, reach_out)
+        return_tiles(0, summed)
+        out_ref[0, H + 1] = summed
 
     @pl.when(inner_above)
     def _():
-        rows_down(1).wait_recv()
-        out_ref[0, H + 2] = rows_in[1]
-
-    @pl.when(jnp.logical_not(inner_above))
-    def _():
-        out_ref[0, H + 2] = zero
+        rows_down().wait_recv()
+        out_ref[0, H + 2] = rows_in[...]
 
     @pl.when(inner_below)
     def _():
-        for d in range(n_smp):
-            back_to(d).wait_recv()
-        out_ref[0, H - 2] = gathered(back_in)
-
-    @pl.when(jnp.logical_not(inner_below))
-    def _():
-        out_ref[0, H - 2] = zero
-
-    @pl.when(above)
+        out_ref[0, H - 2] = gathered(1)
+
+    @pl.when(below)
+    def _():
+        out_ref[0, H - 1] = gathered(0)
+
+    @pl.when(inner_above)
     def _():
         reach_up().wait_send()
 
@@ -318,21 +306,22 @@
         def _(k):
             data_up(k).wait_send()
 
-    @pl.when(inner_below)
+    @pl.when(below)
     def _():
         @pl.loop(0, CHUNKS)
         def _(k):
             data_down(k).wait_send()
 
-    @pl.when(below)
-    def _():
-        rows_down(0).wait_send()
+    @pl.when(above)
+    def _():
+        for d in range(n_smp):
+            tiles_up(0, d).wait_send()
 
     @pl.when(inner)
     def _():
-        rows_down(1).wait_send()
-        for d in range(n_smp):
-            back_to(d).wait_send()
+        rows_down().wait_send()
+        for d in range(n_smp):
+            tiles_up(1, d).wait_send()
 
 
 def solution(mesh):
@@ -368,12 +357,10 @@
                 pltpu.VMEM((2, width, width), f32),
                 pltpu.VMEM((2, width, width), bf16),
                 pltpu.VMEM((2, n_smp - 1, rows, width), bf16),
-                pltpu.VMEM((2, rows, width), f32),
-                pltpu.VMEM((2, rows, width), f32),
-                pltpu.VMEM((n_smp, rows, rows), bf16),
-                pltpu.VMEM((n_smp, rows, rows), bf16),
-                pltpu.VMEM((n_smp, rows, rows), bf16),
-                pltpu.VMEM((n_smp, rows, rows), bf16),
+                pltpu.VMEM((rows, width), f32),
+                pltpu.VMEM((rows, width), f32),
+                pltpu.VMEM((2, n_smp, rows, rows), bf16),
+                pltpu.VMEM((2, n_smp, rows, rows), bf16),
                 dma((3,)),
                 dma((CHUNKS,)),
                 dma((2, CHUNKS)),
@@ -382,12 +369,11 @@
                 dma((2, n_smp - 1)),
                 dma((2, 2, n_smp - 1)),
                 dma((2, 2, n_smp - 1)),
-                dma((2, 2)),
-                dma((2, n_smp - 1)),
-                dma((2, n_smp)),
+                dma((2,)),
+                dma((2, 2, n_smp)),
             ],
             compiler_params=pltpu.CompilerParams(
-                collective_id=0, has_side_effects=True, vmem_limit_bytes=40 << 20
+                collective_id=0, has_side_effects=True, vmem_limit_bytes=62 << 20
             ),
         )(allele_counts[None], keep[None], reach, dosage)
 

time: 112 us -> 109 us (0.973)
  local copies, waits for them, and re-layouts: 4.26 us -> 1.72 us
    unnamed x7 -> x1, local copies, waits for them, and re-layouts: 4.26 us -> 1.72 us
where the time goes in v3:
time: 109 us
  Pallas kernels  106 us (97%)
  local copies, waits for them, and re-layouts  1.72 us (2%)
    pallas_call x1, Pallas kernels, on_device(): pl.pallas_call(functools.partial(kernel, n_blk, n_smp, samples * n_smp),...  106 us

profile of v3, /device:TPU:0, one launch (start us, length us, event | category | flops | bytes accessed | tf_op | source)
XLA Modules:
  0.0 108.5 jit_solution(15656152743491805417)
XLA Ops:
  0.7 106.2 %shard_map.46 = f32[1,5,64,256]{3,2,1,0:T(8,128)} custom-call(s32[1,256]{1,0:T(1,128)} %bitcast.2, f32[1,256]{1,0:T(1,128)} %bitcast.3, s32[1]{0:T(128)S(6)} %copy.6.reach_hbm, bf16[8192,256]{1,0:T(8,128)(2,1)} %dosage_ref.1), custom_call_target="tpu_custom_call" | custom-call | tf_op jit(solution)/shard_map/pallas_call | solution.py:338
  106.8 1.7 %copy.7 = f32[1,5,64,256]{3,2,1,0:T(8,128)} copy(f32[1,5,64,256]{3,2,1,0:T(8,128)} %shard_map.46) | data formatting | bytes 655360

commit v4 on v3

--- a/solution.py
+++ b/solution.py
@@ -86,11 +86,11 @@
     def rows_down():
         return remote(rows_out, rows_in, rows_sem.at[0], rows_sem.at[1], blk=z - 1)
 
-    def tiles_up(j, d):
+    def tiles_up(d):
         p = peer_of(d)
         return remote(
-            tiles_out.at[j, p], tiles_in.at[j, s],
-            tiles_sem.at[0, j, d], tiles_sem.at[1, j, d], blk=z + 1, smp=p,
+            tiles_out.at[p], tiles_in.at[s],
+            tiles_sem.at[0, d], tiles_sem.at[1, d], blk=z + 1, smp=p,
         )
 
     metas = [
@@ -169,6 +169,7 @@
         diag_to(d).start()
 
     zero = jnp.zeros((rows, width), jnp.float32)
+    rows_out[...] = zero
     acc[...] = jnp.zeros_like(acc)
     late[...] = jnp.zeros_like(late)
 
@@ -222,20 +223,6 @@
         summed = jnp.where(limit[0:1, 0:1] >= j + 1.0, summed / total, 0.0)
         return summed
 
-    def return_tiles(j, summed):
-        turned = summed.T.astype(jnp.bfloat16)
-        for p in range(n_smp):
-            tiles_out[j, p] = turned[p * rows : (p + 1) * rows]
-        for d in range(n_smp):
-            tiles_up(j, d).start()
-
-    def gathered(j):
-        for d in range(n_smp):
-            tiles_up(j, d).wait_recv()
-        return jnp.concatenate(
-            [tiles_in[j, q].astype(jnp.float32) for q in range(n_smp)], axis=1
-        )
-
     @pl.when(jnp.logical_not(above))
     def _():
         out_ref[0, H + 1] = zero
@@ -276,27 +263,33 @@
 
         @pl.when(inner)
         def _():
-            summed = late_sum(1, reach_in)
-            rows_out[...] = summed
+            rows_out[...] = late_sum(1, reach_in)
             rows_down().start()
-            return_tiles(1, summed)
 
         summed = late_sum(0, reach_out)
-        return_tiles(0, summed)
         out_ref[0, H + 1] = summed
+        both = jnp.concatenate([summed, rows_out[...]], axis=0)
+        turned = both.T.astype(jnp.bfloat16)
+        for p in range(n_smp):
+            tiles_out[p] = turned[p * rows : (p + 1) * rows]
+        for d in range(n_smp):
+            tiles_up(d).start()
 
     @pl.when(inner_above)
     def _():
         rows_down().wait_recv()
         out_ref[0, H + 2] = rows_in[...]
 
-    @pl.when(inner_below)
-    def _():
-        out_ref[0, H - 2] = gathered(1)
-
     @pl.when(below)
     def _():
-        out_ref[0, H - 1] = gathered(0)
+        for d in range(n_smp):
+            tiles_up(d).wait_recv()
+        tiles = [tiles_in[q].astype(jnp.float32) for q in range(n_smp)]
+        out_ref[0, H - 1] = jnp.concatenate([tile[:, :rows] for tile in tiles], axis=1)
+
+        @pl.when(inner_below)
+        def _():
+            out_ref[0, H - 2] = jnp.concatenate([tile[:, rows:] for tile in tiles], axis=1)
 
     @pl.when(inner_above)
     def _():
@@ -315,13 +308,11 @@
     @pl.when(above)
     def _():
         for d in range(n_smp):
-            tiles_up(0, d).wait_send()
+            tiles_up(d).wait_send()
 
     @pl.when(inner)
     def _():
         rows_down().wait_send()
-        for d in range(n_smp):
-            tiles_up(1, d).wait_send()
 
 
 def solution(mesh):
@@ -359,8 +350,8 @@
                 pltpu.VMEM((2, n_smp - 1, rows, width), bf16),
                 pltpu.VMEM((rows, width), f32),
                 pltpu.VMEM((rows, width), f32),
-                pltpu.VMEM((2, n_smp, rows, rows), bf16),
-                pltpu.VMEM((2, n_smp, rows, rows), bf16),
+                pltpu.VMEM((n_smp, rows, 2 * rows), bf16),
+                pltpu.VMEM((n_smp, rows, 2 * rows), bf16),
                 dma((3,)),
                 dma((CHUNKS,)),
                 dma((2, CHUNKS)),
@@ -370,7 +361,7 @@
                 dma((2, 2, n_smp - 1)),
                 dma((2, 2, n_smp - 1)),
                 dma((2,)),
-                dma((2, 2, n_smp)),
+                dma((2, n_smp)),
             ],
             compiler_params=pltpu.CompilerParams(
                 collective_id=0, has_side_effects=True, vmem_limit_bytes=62 << 20

time: 109 us -> 109 us (level)
  no operation moved by 1% of the time
where the time goes in v4:
time: 109 us; the launch traced here: 108 us
  Pallas kernels  106 us (97%)
  local copies, waits for them, and re-layouts  1.72 us (2%)
    pallas_call x1, Pallas kernels, on_device(): pl.pallas_call(functools.partial(kernel, n_blk, n_smp, samples * n_smp),...  106 us

profile of v4, /device:TPU:0, one launch (start us, length us, event | category | flops | bytes accessed | tf_op | source)
XLA Modules:
  0.0 108.5 jit_solution(1358587702241199719)
XLA Ops:
  0.7 106.1 %shard_map.46 = f32[1,5,64,256]{3,2,1,0:T(8,128)} custom-call(s32[1,256]{1,0:T(1,128)} %bitcast.2, f32[1,256]{1,0:T(1,128)} %bitcast.3, s32[1]{0:T(128)S(6)} %copy.6.reach_hbm, bf16[8192,256]{1,0:T(8,128)(2,1)} %dosage_ref.1), custom_call_target="tpu_custom_call" | custom-call | tf_op jit(solution)/shard_map/pallas_call | solution.py:329
  106.7 1.7 %copy.7 = f32[1,5,64,256]{3,2,1,0:T(8,128)} copy(f32[1,5,64,256]{3,2,1,0:T(8,128)} %shard_map.46) | data formatting | bytes 655360
